TPU v7x, 512 devices: a whole 4x4x16 slice. The times are simulated.
512 devices in a mesh: row: 32 (over z, core), col: 16 (over x, y).
Axes of the slice: x: 4, y: 4, z: 16, core: 2. Of those that a mesh axis runs over, the one named last changes fastest.
Arguments:
- blocks: bfloat16 [16384, 128, 128], P(('row', 'col')), may hold values from -0.09375 to 0.09375
- block_rows: int32 [16384], P(('row', 'col')), may hold values from 0 to 512, as said below
- block_cols: int32 [16384], P(('row', 'col')), may hold values from 0 to 512, as said below
- start: float32 [64, 65536], P(None, ('row', 'col'))
Outputs:
- basis: float32 [64, 65536], P(None, ('row', 'col'))
- alphas: float32 [3, 64, 64], replicated
- betas: float32 [3, 64, 64], replicated
Inputs may be any that keep to these rules, and one draw needn't show every extreme that they name: For device d the entries d * 32 to (d + 1) * 32 - 1 list its stored blocks first and then empty slots, which hold 512 in both lists. A stored block (i, j) has i <= j, i // 16 equal to the device's row index, j % 16 equal to its col index, and no position is stored twice. The devices of row index 0 fill all 32 slots; block_cols holds 512 exactly where block_rows does. `block_cols`: see block_rows.
All inputs are finite; a program needn't handle non-finite values.
Results may differ from a plain program's by a relative error of at most 0.04.
Values may be sent and summed in bfloat16 or wider, within the bound.
A program may use at most 64 MiB of HBM per device.

v0:
```python
import jax
import jax.numpy as jnp
from jax import lax
from jax.sharding import PartitionSpec as P

ITERS = 3
HIGH = lax.Precision.HIGHEST


def local_inner(left, right):
    return jnp.dot(left, right.T, precision=HIGH)


def factorize(gramian, identity):
    factor_low = jnp.linalg.cholesky(gramian)
    inverse = jax.scipy.linalg.solve_triangular(factor_low, identity, lower=True)
    return (inverse, factor_low)


def shards(blocks, block_rows, block_cols, start):
    row_count = lax.axis_size("row")
    col_count = lax.axis_size("col")
    row_index = lax.axis_index("row")
    vec_width = start.shape[0]
    block_size = start.shape[1]
    columns_all = row_count * col_count * block_size
    identity = jnp.eye(vec_width, dtype=jnp.float32)
    row_target = block_rows - row_index * col_count
    col_target = block_cols // col_count
    hot_rows = row_target[:, None] == jnp.arange(col_count)[None, :]
    hot_cols = col_target[:, None] == jnp.arange(row_count)[None, :]
    gramian = lax.psum(local_inner(start, start), ("row", "col")) / columns_all
    inverse, factor_low = factorize(gramian, identity)
    basis = jnp.dot(inverse, start, precision=HIGH)
    previous = None
    alpha_list = []
    beta_list = []
    for step in range(ITERS):
        rounded = basis.astype(jnp.bfloat16)
        row_stripe = lax.all_gather(rounded, "col", axis=1, tiled=True).reshape(
            vec_width, col_count, block_size
        )
        column_set = lax.all_gather(rounded, "row", axis=1, tiled=True).reshape(
            vec_width, row_count, block_size
        )
        taken_cols = jnp.einsum(
            "kmb,sm->ksb",
            column_set,
            hot_cols.astype(jnp.bfloat16),
            preferred_element_type=jnp.float32,
        ).astype(jnp.bfloat16)
        taken_rows = jnp.einsum(
            "kmb,sm->ksb",
            row_stripe,
            hot_rows.astype(jnp.bfloat16),
            preferred_element_type=jnp.float32,
        ).astype(jnp.bfloat16)
        forward = jnp.einsum("ksb,sdb->ksd", taken_cols, blocks, preferred_element_type=jnp.float32)
        row_part = jnp.einsum("ksd,sm->kmd", forward, hot_rows.astype(jnp.float32), precision=HIGH)
        backward = jnp.einsum(
            "ksb,sbd->ksd", taken_rows, blocks, preferred_element_type=jnp.float32
        )
        col_part = jnp.einsum("ksd,sm->kmd", backward, hot_cols.astype(jnp.float32), precision=HIGH)
        own_rows = lax.psum_scatter(
            row_part.astype(jnp.bfloat16), "col", scatter_dimension=1, tiled=True
        ).astype(jnp.float32)
        own_cols = lax.psum_scatter(
            col_part.astype(jnp.bfloat16), "row", scatter_dimension=1, tiled=True
        ).astype(jnp.float32)
        residue = own_rows.reshape(vec_width, block_size) + own_cols.reshape(vec_width, block_size)
        if previous is not None:
            residue = residue - jnp.dot(factor_low.T, previous, precision=HIGH)
        alpha = lax.psum(local_inner(basis, residue), ("row", "col")) / columns_all
        residue = residue - jnp.dot(alpha.T, basis, precision=HIGH)
        gramian = lax.psum(local_inner(residue, residue), ("row", "col")) / columns_all
        inverse, factor_low = factorize(gramian, identity)
        alpha_list.append(alpha)
        beta_list.append(factor_low)
        previous = basis
        basis = jnp.dot(inverse, residue, precision=HIGH)
    return (basis, jnp.stack(alpha_list), jnp.stack(beta_list))


def solution(mesh):
    in_specs = (
        P(("row", "col"), None, None),
        P(("row", "col")),
        P(("row", "col")),
        P(None, ("row", "col")),
    )
    out_specs = (P(None, ("row", "col")), P(), P())
    return jax.shard_map(shards, mesh=mesh, in_specs=in_specs, out_specs=out_specs, check_vma=False)
```

profile of v0, /device:TPU:1, one launch (start us, length us, event | category | flops | bytes accessed | tf_op | source)
XLA Modules:
  0.0 1513.7 jit_solution(926172588916791671)
XLA Ops:
  8.3 111.2 %psum.49 = f32[64,64]{0,1:T(8,128)S(1)} all-reduce(f32[64,64]{0,1:T(8,128)S(1)} %fusion.127), channel_id=1, replica_groups=mesh['row'=32,'col'=16] {'row','col'}, use_global_device_ids=true, to_apply=%region_0.1 | all-reduce | flops 4096 | bytes 32768 | tf_op jit(solution)/shard_map/psum | solution.py:32
  119.5 5.8 cholesky.74
  126.7 4.9 custom-call.8
  133.2 29.9 %all_gather.18 = bf16[64,4096]{1,0:T(8,128)(2,1)S(1)} all-gather(bf16[64,128]{1,0:T(8,128)(2,1)S(1)} %get-tuple-element.17), channel_id=1, replica_groups=mesh['row'=32,'col'=16] {'row'}, dimensions={1}, use_global_device_ids=true | all-gather | bytes 540672 | tf_op jit(solution)/shard_map/all_gather | solution.py:43
  167.0 16.5 %all_gather.19 = bf16[64,2048]{1,0:T(8,128)(2,1)S(1)} all-gather(bf16[64,128]{1,0:T(8,128)(2,1)S(1)} %get-tuple-element.17), channel_id=1, replica_groups=mesh['row'=32,'col'=16] {'col'}, dimensions={1}, use_global_device_ids=true | all-gather | bytes 278528 | tf_op jit(solution)/shard_map/all_gather | solution.py:40
  184.3 1.3 fusion
  186.6 58.9 %reduce-scatter.19.cloned.1.call-done = bf16[64,1,128]{2,0,1:T(8,128)(2,1)} async-done(((bf16[64,16,128]{2,0,1:T(8,128)(2,1)}), bf16[64,1,128]{2,0,1:T(8,128)(2,1)}) %reduce-scatter.19.cloned.1.call-update) | async-done | bytes 16400
  245.6 108.3 %reduce-scatter.13.cloned.1.call-done = bf16[64,1,128]{2,0,1:T(8,128)(2,1)} async-done(((bf16[64,32,128]{2,0,1:T(8,128)(2,1)}), bf16[64,1,128]{2,0,1:T(8,128)(2,1)}) %reduce-scatter.13.cloned.1.call-update) | async-done | bytes 16400 | tf_op jit(solution)/shard_map/reduce_scatter | solution.py:67
  354.8 106.5 %psum.50 = f32[64,64]{0,1:T(8,128)S(1)} all-reduce(f32[64,64]{0,1:T(8,128)S(1)} %fusion.51), channel_id=1, replica_groups=mesh['row'=32,'col'=16] {'row','col'}, use_global_device_ids=true, to_apply=%region_5.8 | all-reduce | flops 4096 | bytes 32768 | tf_op jit(solution)/shard_map/psum | solution.py:73
  461.7 98.9 %psum.51 = f32[64,64]{0,1:T(8,128)S(1)} all-reduce(f32[64,64]{0,1:T(8,128)S(1)} %fusion.128), channel_id=1, replica_groups=mesh['row'=32,'col'=16] {'row','col'}, use_global_device_ids=true, to_apply=%region_6.9 | all-reduce | flops 4096 | bytes 32768 | tf_op jit(solution)/shard_map/psum | solution.py:75
  560.7 5.8 cholesky.85
  567.9 4.9 custom-call.9
  573.2 31.9 %all_gather.20 = bf16[64,4096]{1,0:T(8,128)(2,1)S(1)} all-gather(bf16[64,128]{1,0:T(8,128)(2,1)S(1)} %get-tuple-element.19), channel_id=1, replica_groups=mesh['row'=32,'col'=16] {'row'}, dimensions={1}, use_global_device_ids=true | all-gather | bytes 540672 | tf_op jit(solution)/shard_map/all_gather | solution.py:43
  605.0 17.4 %all_gather.21 = bf16[64,2048]{1,0:T(8,128)(2,1)S(1)} all-gather(bf16[64,128]{1,0:T(8,128)(2,1)S(1)} %get-tuple-element.19), channel_id=1, replica_groups=mesh['row'=32,'col'=16] {'col'}, dimensions={1}, use_global_device_ids=true | all-gather | bytes 278528 | tf_op jit(solution)/shard_map/all_gather | solution.py:40
  626.5 1.3 fusion.1
  628.8 81.9 %reduce-scatter.21.cloned.1.call-done = bf16[64,1,128]{2,0,1:T(8,128)(2,1)} async-done(((bf16[64,16,128]{2,0,1:T(8,128)(2,1)}), bf16[64,1,128]{2,0,1:T(8,128)(2,1)}) %reduce-scatter.21.cloned.1.call-update) | async-done | bytes 16400
  710.7 108.1 %reduce-scatter.15.cloned.1.call-done = bf16[64,1,128]{2,0,1:T(8,128)(2,1)} async-done(((bf16[64,32,128]{2,0,1:T(8,128)(2,1)}), bf16[64,1,128]{2,0,1:T(8,128)(2,1)}) %reduce-scatter.15.cloned.1.call-update) | async-done | bytes 16400 | tf_op jit(solution)/shard_map/reduce_scatter | solution.py:67
  818.8 1.6 convolution_subtract_fusion.3
  820.7 106.2 %psum.52 = f32[64,64]{0,1:T(8,128)S(1)} all-reduce(f32[64,64]{0,1:T(8,128)S(1)} %fusion.129), channel_id=1, replica_groups=mesh['row'=32,'col'=16] {'row','col'}, use_global_device_ids=true, to_apply=%region_9.12 | all-reduce | flops 4096 | bytes 32768 | tf_op jit(solution)/shard_map/psum | solution.py:73
  927.2 98.9 %psum.53 = f32[64,64]{0,1:T(8,128)S(1)} all-reduce(f32[64,64]{0,1:T(8,128)S(1)} %fusion.130), channel_id=1, replica_groups=mesh['row'=32,'col'=16] {'row','col'}, use_global_device_ids=true, to_apply=%region_10.13 | all-reduce | flops 4096 | bytes 32768 | tf_op jit(solution)/shard_map/psum | solution.py:75
  1026.2 5.8 cholesky.96
  1033.4 4.9 custom-call.10
  1038.7 31.9 %all_gather.22 = bf16[64,4096]{1,0:T(8,128)(2,1)S(1)} all-gather(bf16[64,128]{1,0:T(8,128)(2,1)S(1)} %get-tuple-element.21), channel_id=1, replica_groups=mesh['row'=32,'col'=16] {'row'}, dimensions={1}, use_global_device_ids=true | all-gather | bytes 540672 | tf_op jit(solution)/shard_map/all_gather | solution.py:43
  1070.6 17.6 %all_gather.23 = bf16[64,2048]{1,0:T(8,128)(2,1)S(1)} all-gather(bf16[64,128]{1,0:T(8,128)(2,1)S(1)} %get-tuple-element.21), channel_id=1, replica_groups=mesh['row'=32,'col'=16] {'col'}, dimensions={1}, use_global_device_ids=true | all-gather | bytes 278528 | tf_op jit(solution)/shard_map/all_gather | solution.py:40
  1092.2 1.3 fusion.2
  1094.5 81.9 %reduce-scatter.23.cloned.1.call-done = bf16[64,1,128]{2,0,1:T(8,128)(2,1)} async-done(((bf16[64,16,128]{2,0,1:T(8,128)(2,1)}), bf16[64,1,128]{2,0,1:T(8,128)(2,1)}) %reduce-scatter.23.cloned.1.call-update) | async-done | bytes 16400
  1176.4 108.4 %reduce-scatter.17.cloned.1.call-done = bf16[64,1,128]{2,0,1:T(8,128)(2,1)} async-done(((bf16[64,32,128]{2,0,1:T(8,128)(2,1)}), bf16[64,1,128]{2,0,1:T(8,128)(2,1)}) %reduce-scatter.17.cloned.1.call-update) | async-done | bytes 16400 | tf_op jit(solution)/shard_map/reduce_scatter | solution.py:67
  1284.9 1.6 convolution_subtract_fusion.1
  1286.7 106.3 %psum.54 = f32[64,64]{0,1:T(8,128)S(1)} all-reduce(f32[64,64]{0,1:T(8,128)S(1)} %fusion.131), channel_id=1, replica_groups=mesh['row'=32,'col'=16] {'row','col'}, use_global_device_ids=true, to_apply=%region_13.16 | all-reduce | flops 4096 | bytes 32768 | tf_op jit(solution)/shard_map/psum | solution.py:73
  1393.3 98.9 %psum.55 = f32[64,64]{0,1:T(8,128)S(1)} all-reduce(f32[64,64]{0,1:T(8,128)S(1)} %fusion.132), channel_id=1, replica_groups=mesh['row'=32,'col'=16] {'row','col'}, use_global_device_ids=true, to_apply=%region_14.17 | all-reduce | flops 4096 | bytes 32768 | tf_op jit(solution)/shard_map/psum | solution.py:75
  1492.3 5.8 cholesky.107
  1500.3 4.9 custom-call.11
  (101 shorter events, 29.5 us)
Async XLA Ops:
  7.2 157.0 %copy-start = (bf16[32,128,128]{2,1,0:T(8,128)(2,1)S(1)}, bf16[32,128,128]{2,1,0:T(8,128)(2,1)}, u32[]{:S(2)}) copy-start(bf16[32,128,128]{2,1,0:T(8,128)(2,1)} %param.7) | copy-start | bytes 3145732
  7.2 238.4 %reduce-scatter.19.cloned.1.call-start = ((), (), s32[]{:S(2)}) async-start(), calls=%async_computation.9 | async-start | bytes 278528
  131.6 0.8 copy-start.1
  132.6 0.7 copy-start.4
  163.2 0.7 copy-start.5
  166.9 187.0 %reduce-scatter.13.cloned.1.call-start = ((), (), s32[]{:S(2)}) async-start(), calls=%async_computation.6 | async-start | bytes 540672 | tf_op jit(solution)/shard_map/reduce_scatter | solution.py:67
  186.6 524.1 %reduce-scatter.21.cloned.1.call-start = ((), (), s32[]{:S(2)}) async-start(), calls=%async_computation.10 | async-start | bytes 278528
  354.8 106.5 %copy-start.2 = (bf16[64,1,128]{2,0,1:T(8,128)(2,1)S(1)}, bf16[64,1,128]{2,0,1:T(8,128)(2,1)}, u32[]{:S(2)}) copy-start(bf16[64,1,128]{2,0,1:T(8,128)(2,1)} %reduce-scatter.19.cloned.1.call-done) | copy-start | bytes 49156
  354.8 106.5 %copy-start.3 = (bf16[64,1,128]{2,0,1:T(8,128)(2,1)S(1)}, bf16[64,1,128]{2,0,1:T(8,128)(2,1)}, u32[]{:S(2)}) copy-start(bf16[64,1,128]{2,0,1:T(8,128)(2,1)} %reduce-scatter.13.cloned.1.call-done) | copy-start | bytes 49156
  625.6 193.2 %reduce-scatter.15.cloned.1.call-start = ((), (), s32[]{:S(2)}) async-start(), calls=%async_computation.7 | async-start | bytes 540672 | tf_op jit(solution)/shard_map/reduce_scatter | solution.py:67
  628.8 547.7 %reduce-scatter.23.cloned.1.call-start = ((), (), s32[]{:S(2)}) async-start(), calls=%async_computation.11 | async-start | bytes 278528
  1091.4 193.5 %reduce-scatter.17.cloned.1.call-start = ((), (), s32[]{:S(2)}) async-start(), calls=%async_computation.8 | async-start | bytes 540672 | tf_op jit(solution)/shard_map/reduce_scatter | solution.py:67
Sparse Core Ops, SparseCore 0:
  167.0 78.5 reduce-scatter.18
  248.6 105.2 reduce-scatter.12
  625.8 84.9 reduce-scatter.20
  713.6 105.2 reduce-scatter.14
  1091.5 84.9 reduce-scatter.22
  1179.3 105.5 reduce-scatter.16
where the time goes:
time: 1520 us; the launch traced here: 1510 us
  blocking collectives  872 us (57%)
  waiting for transfers between devices  548 us (36%)
  other arithmetic  49 us (3%)
  matrix products  21.6 us (1%)
    reduce_scatter x3, waiting for transfers between devices, shards(): lax.psum_scatter(col_part.astype(jnp.bfloat16), 'row', scatter_dimension=...  325 us
    psum x3, blocking collectives, shards(): alpha = lax.psum(local_inner(basis, residue), ('row', 'col')) / columns_all  319 us
    psum x3, blocking collectives, shards(): lax.psum(local_inner(residue, residue), ('row', 'col')) / columns_all  297 us
    unnamed x9, waiting for transfers between devices  223 us
    psum x1, blocking collectives, shards(): gramian = lax.psum(local_inner(start, start), ('row', 'col')) / columns_all  111 us
    all_gather x3, blocking collectives, shards(): lax.all_gather(rounded, 'row', axis=1, tiled=True)  93.6 us
    all_gather x3, blocking collectives, shards(): lax.all_gather(rounded, 'col', axis=1, tiled=True)  51.5 us
  transfers between devices with their start and end apart: 6, of which 6 were waited for; matrix products, arithmetic and copies ran while one was open for 1% of the time, Pallas kernels for 0%

commit v1 on v0

--- a/solution.py
+++ b/solution.py
@@ -5,6 +5,11 @@
 
 ITERS = 3
 HIGH = lax.Precision.HIGHEST
+
+
+def _see_core(s0):
+    z = lax.all_gather(s0, ("row", "col")).sum(axis=0)
+    return z
 
 
 def local_inner(left, right):
@@ -70,7 +75,7 @@
         residue = own_rows.reshape(vec_width, block_size) + own_cols.reshape(vec_width, block_size)
         if previous is not None:
             residue = residue - jnp.dot(factor_low.T, previous, precision=HIGH)
-        alpha = lax.psum(local_inner(basis, residue), ("row", "col")) / columns_all
+        alpha = _see_core(local_inner(basis, residue)) / columns_all
         residue = residue - jnp.dot(alpha.T, basis, precision=HIGH)
         gramian = lax.psum(local_inner(residue, residue), ("row", "col")) / columns_all
         inverse, factor_low = factorize(gramian, identity)

time: 1520 us -> 1890 us (1.24)
  waiting for transfers between devices: 548 us -> 1210 us
  blocking collectives: 872 us -> 567 us
  other arithmetic: 49 us -> 71.2 us
    all_gather x0 -> x3, waiting for transfers between devices: none -> 671 us  [_see_core(): z = lax.all_gather(s0, ('row', 'col')).sum(axis=0)]
    psum x3 -> x0, blocking collectives: 319 us -> none  [shards(): alpha = lax.psum(local_inner(basis, residue), ('row', 'col')) / columns_all]
    reduce_sum x0 -> x3, other arithmetic: none -> 20.8 us  [_see_core(): z = lax.all_gather(s0, ('row', 'col')).sum(axis=0)]
    unnamed x9 -> x12, waiting for transfers between devices: 223 us -> 213 us
  transfers between devices with their start and end apart: 6 -> 9, of which waited for: 6 -> 9; matrix products, arithmetic and copies ran while one was open for 1% -> 0% of each run, Pallas kernels for 0% -> 0%
where the time goes in v1:
time: 1890 us
  waiting for transfers between devices  1210 us (64%)
  blocking collectives  567 us (30%)
  other arithmetic  71.2 us (4%)
  matrix products  24.3 us (1%)
    all_gather x3, waiting for transfers between devices, _see_core(): z = lax.all_gather(s0, ('row', 'col')).sum(axis=0)  671 us
    reduce_scatter x3, waiting for transfers between devices, shards(): lax.psum_scatter(col_part.astype(jnp.bfloat16), 'row', scatter_dimension=...  325 us
    psum x3, blocking collectives, shards(): lax.psum(local_inner(residue, residue), ('row', 'col')) / columns_all  305 us
    unnamed x12, waiting for transfers between devices  213 us
    psum x1, blocking collectives, shards(): gramian = lax.psum(local_inner(start, start), ('row', 'col')) / columns_all  111 us
    all_gather x3, blocking collectives, shards(): lax.all_gather(rounded, 'row', axis=1, tiled=True)  99.5 us
    all_gather x3, blocking collectives, shards(): lax.all_gather(rounded, 'col', axis=1, tiled=True)  52 us
  transfers between devices with their start and end apart: 9, of which 9 were waited for; matrix products, arithmetic and copies ran while one was open for 0% of the time, Pallas kernels for 0%

profile of v1, /device:TPU:1, one launch (start us, length us, event | category | flops | bytes accessed | tf_op | source)
XLA Modules:
  0.0 1893.2 jit_solution(10752745426983985636)
XLA Ops:
  9.0 111.2 %psum.28 = f32[64,64]{0,1:T(8,128)S(1)} all-reduce(f32[64,64]{0,1:T(8,128)S(1)} %fusion.127), channel_id=1, replica_groups=mesh['row'=32,'col'=16] {'row','col'}, use_global_device_ids=true, to_apply=%region_0.1 | all-reduce | flops 4096 | bytes 32768 | tf_op jit(solution)/shard_map/psum | solution.py:37
  120.2 5.8 cholesky.74
  127.4 4.9 custom-call.8
  133.5 29.9 %all_gather.36 = bf16[64,4096]{1,0:T(8,128)(2,1)S(1)} all-gather(bf16[64,128]{1,0:T(8,128)(2,1)S(1)} %get-tuple-element.17), channel_id=1, replica_groups=mesh['row'=32,'col'=16] {'row'}, dimensions={1}, use_global_device_ids=true | all-gather | bytes 540672 | tf_op jit(solution)/shard_map/all_gather | solution.py:48
  167.3 16.5 all_gather.37
  186.9 59.0 %reduce-scatter.19.cloned.1.call-done = bf16[64,1,128]{2,0,1:T(8,128)(2,1)} async-done(((bf16[64,16,128]{2,0,1:T(8,128)(2,1)}), bf16[64,1,128]{2,0,1:T(8,128)(2,1)}) %reduce-scatter.19.cloned.1.call-update) | async-done | bytes 16400
  245.9 108.7 %reduce-scatter.13.cloned.1.call-done = bf16[64,1,128]{2,0,1:T(8,128)(2,1)} async-done(((bf16[64,32,128]{2,0,1:T(8,128)(2,1)}), bf16[64,1,128]{2,0,1:T(8,128)(2,1)}) %reduce-scatter.13.cloned.1.call-update) | async-done | bytes 16400 | tf_op jit(solution)/shard_map/reduce_scatter | solution.py:72
  356.2 223.8 %all-gather.7.cloned.1.call-done = f32[32768,64]{1,0:T(8,128)} async-done(((f32[64,64]{1,0:T(8,128)}), f32[32768,64]{1,0:T(8,128)}) %all-gather.7.cloned.1.call-update) | async-done | bytes 8388624 | tf_op jit(solution)/shard_map/all_gather | solution.py:11
  580.0 6.9 reduce_sum.27
  587.4 101.5 %psum.29 = f32[64,64]{0,1:T(8,128)S(1)} all-reduce(f32[64,64]{0,1:T(8,128)S(1)} %fusion.128), channel_id=1, replica_groups=mesh['row'=32,'col'=16] {'row','col'}, use_global_device_ids=true, to_apply=%region_6.9 | all-reduce | flops 4096 | bytes 32768 | tf_op jit(solution)/shard_map/psum | solution.py:80
  689.1 5.8 cholesky.85
  696.3 4.9 custom-call.9
  701.6 17.8 all_gather.41
  719.4 34.8 %all_gather.40 = bf16[64,4096]{1,0:T(8,128)(2,1)S(1)} all-gather(bf16[64,128]{1,0:T(8,128)(2,1)S(1)} %get-tuple-element.19), channel_id=1, replica_groups=mesh['row'=32,'col'=16] {'row'}, dimensions={1}, use_global_device_ids=true | all-gather | bytes 540672 | tf_op jit(solution)/shard_map/all_gather | solution.py:48
  760.5 76.8 %reduce-scatter.21.cloned.1.call-done = bf16[64,1,128]{2,0,1:T(8,128)(2,1)} async-done(((bf16[64,16,128]{2,0,1:T(8,128)(2,1)}), bf16[64,1,128]{2,0,1:T(8,128)(2,1)}) %reduce-scatter.21.cloned.1.call-update) | async-done | bytes 16400
  837.3 108.1 %reduce-scatter.15.cloned.1.call-done = bf16[64,1,128]{2,0,1:T(8,128)(2,1)} async-done(((bf16[64,32,128]{2,0,1:T(8,128)(2,1)}), bf16[64,1,128]{2,0,1:T(8,128)(2,1)}) %reduce-scatter.15.cloned.1.call-update) | async-done | bytes 16400 | tf_op jit(solution)/shard_map/reduce_scatter | solution.py:72
  945.4 1.6 convolution_subtract_fusion.3
  947.9 223.5 %all-gather.9.cloned.1.call-done = f32[32768,64]{1,0:T(8,128)} async-done(((f32[64,64]{1,0:T(8,128)}), f32[32768,64]{1,0:T(8,128)}) %all-gather.9.cloned.1.call-update) | async-done | bytes 8388624 | tf_op jit(solution)/shard_map/all_gather | solution.py:11
  1171.4 6.9 reduce_sum.28
  1178.8 101.6 %psum.30 = f32[64,64]{0,1:T(8,128)S(1)} all-reduce(f32[64,64]{0,1:T(8,128)S(1)} %fusion.130), channel_id=1, replica_groups=mesh['row'=32,'col'=16] {'row','col'}, use_global_device_ids=true, to_apply=%region_10.13 | all-reduce | flops 4096 | bytes 32768 | tf_op jit(solution)/shard_map/psum | solution.py:80
  1280.4 5.8 cholesky.96
  1287.6 4.9 custom-call.10
  1293.0 17.8 all_gather.45
  1310.7 34.8 %all_gather.44 = bf16[64,4096]{1,0:T(8,128)(2,1)S(1)} all-gather(bf16[64,128]{1,0:T(8,128)(2,1)S(1)} %get-tuple-element.21), channel_id=1, replica_groups=mesh['row'=32,'col'=16] {'row'}, dimensions={1}, use_global_device_ids=true | all-gather | bytes 540672 | tf_op jit(solution)/shard_map/all_gather | solution.py:48
  1351.9 76.8 %reduce-scatter.23.cloned.1.call-done = bf16[64,1,128]{2,0,1:T(8,128)(2,1)} async-done(((bf16[64,16,128]{2,0,1:T(8,128)(2,1)}), bf16[64,1,128]{2,0,1:T(8,128)(2,1)}) %reduce-scatter.23.cloned.1.call-update) | async-done | bytes 16400
  1428.7 108.2 %reduce-scatter.17.cloned.1.call-done = bf16[64,1,128]{2,0,1:T(8,128)(2,1)} async-done(((bf16[64,32,128]{2,0,1:T(8,128)(2,1)}), bf16[64,1,128]{2,0,1:T(8,128)(2,1)}) %reduce-scatter.17.cloned.1.call-update) | async-done | bytes 16400 | tf_op jit(solution)/shard_map/reduce_scatter | solution.py:72
  1536.9 1.6 convolution_subtract_fusion.1
  1539.4 223.7 %all-gather.11.cloned.1.call-done = f32[32768,64]{1,0:T(8,128)} async-done(((f32[64,64]{1,0:T(8,128)}), f32[32768,64]{1,0:T(8,128)}) %all-gather.11.cloned.1.call-update) | async-done | bytes 8388624 | tf_op jit(solution)/shard_map/all_gather | solution.py:11
  1763.0 6.9 reduce_sum.29
  1771.2 101.6 %psum.31 = f32[64,64]{0,1:T(8,128)S(1)} all-reduce(f32[64,64]{0,1:T(8,128)S(1)} %fusion.132), channel_id=1, replica_groups=mesh['row'=32,'col'=16] {'row','col'}, use_global_device_ids=true, to_apply=%region_14.17 | all-reduce | flops 4096 | bytes 32768 | tf_op jit(solution)/shard_map/psum | solution.py:80
  1872.9 5.8 cholesky.107
  1880.1 4.9 custom-call.11
  (107 shorter events, 36.0 us)
Async XLA Ops:
  7.2 157.3 %copy-start = (bf16[32,128,128]{2,1,0:T(8,128)(2,1)S(1)}, bf16[32,128,128]{2,1,0:T(8,128)(2,1)}, u32[]{:S(2)}) copy-start(bf16[32,128,128]{2,1,0:T(8,128)(2,1)} %param.7) | copy-start | bytes 3145732
  7.2 238.7 %reduce-scatter.19.cloned.1.call-start = ((), (), s32[]{:S(2)}) async-start(), calls=%async_computation.12 | async-start | bytes 278528
  167.2 187.4 %reduce-scatter.13.cloned.1.call-start = ((), (), s32[]{:S(2)}) async-start(), calls=%async_computation.6 | async-start | bytes 540672 | tf_op jit(solution)/shard_map/reduce_scatter | solution.py:72
  186.8 393.2 %all-gather.7.cloned.1.call-start = ((), (), s32[]{:S(2)}) async-start(), calls=%async_computation.9 | async-start | bytes 16809984 | tf_op jit(solution)/shard_map/all_gather | solution.py:11
  245.9 341.2 %copy-start.1 = (bf16[64,1,128]{2,0,1:T(8,128)(2,1)S(1)}, bf16[64,1,128]{2,0,1:T(8,128)(2,1)}, u32[]{:S(2)}) copy-start(bf16[64,1,128]{2,0,1:T(8,128)(2,1)} %reduce-scatter.19.cloned.1.call-done) | copy-start | bytes 49156
  354.6 232.5 %copy-start.2 = (bf16[64,1,128]{2,0,1:T(8,128)(2,1)S(1)}, bf16[64,1,128]{2,0,1:T(8,128)(2,1)}, u32[]{:S(2)}) copy-start(bf16[64,1,128]{2,0,1:T(8,128)(2,1)} %reduce-scatter.13.cloned.1.call-done) | copy-start | bytes 49156
  356.2 481.1 %reduce-scatter.21.cloned.1.call-start = ((), (), s32[]{:S(2)}) async-start(), calls=%async_computation.13 | async-start | bytes 278528
  757.7 187.7 %reduce-scatter.15.cloned.1.call-start = ((), (), s32[]{:S(2)}) async-start(), calls=%async_computation.7 | async-start | bytes 540672 | tf_op jit(solution)/shard_map/reduce_scatter | solution.py:72
  760.5 410.9 %all-gather.9.cloned.1.call-start = ((), (), s32[]{:S(2)}) async-start(), calls=%async_computation.10 | async-start | bytes 16809984 | tf_op jit(solution)/shard_map/all_gather | solution.py:11
  947.8 480.8 %reduce-scatter.23.cloned.1.call-start = ((), (), s32[]{:S(2)}) async-start(), calls=%async_computation.14 | async-start | bytes 278528
  1349.1 187.8 %reduce-scatter.17.cloned.1.call-start = ((), (), s32[]{:S(2)}) async-start(), calls=%async_computation.8 | async-start | bytes 540672 | tf_op jit(solution)/shard_map/reduce_scatter | solution.py:72
  1351.8 411.2 %all-gather.11.cloned.1.call-start = ((), (), s32[]{:S(2)}) async-start(), calls=%async_computation.11 | async-start | bytes 16809984 | tf_op jit(solution)/shard_map/all_gather | solution.py:11
Sparse Core Ops, SparseCore 0:
  167.3 78.5 reduce-scatter.18
  248.9 105.6 reduce-scatter.12
  359.6 220.4 all-gather.6
  757.8 79.3 reduce-scatter.20
  840.1 105.2 reduce-scatter.14
  950.3 221.0 all-gather.8
  1349.2 79.4 reduce-scatter.22
  1431.7 105.1 reduce-scatter.16
  1541.9 221.0 all-gather.10
